TPU v7x, 128 devices: a whole 4x4x4 slice. The times are simulated.
128 devices in a mesh: gx: 8 (over z, core), gy: 16 (over y, x).
Axes of the slice: x: 4, y: 4, z: 4, core: 2. Of those that a mesh axis runs over, the one named last changes fastest.
Arguments:
- concentration: float32 [1024, 64, 4096], P(('gx', 'gy')), may hold values from 0.05 to 0.95
- neighbour: int32 [1024, 6], P(('gx', 'gy')), may hold values from -1 to 1023, as said below
- new_owner: int32 [1024], P(('gx', 'gy')), may hold values from -1 to 127, as said below
- new_slot: int32 [1024], P(('gx', 'gy')), may hold values from -1 to 7, as said below
Outputs:
- advanced: float32 [1024, 64, 4096], P(('gx', 'gy'))
Inputs may be any that keep to these rules, and one draw needn't show every extreme that they name: Global slot = device * 8 + slot, devices numbered along gx then gy. The occupied slots of a device are its first ones, between 2 and 8 of them (some device has all 8); empty slots have no neighbours and are nobody's neighbour. The relation is symmetric: if h is beside g in direction d, g is beside h in the opposite direction. Along x a block's neighbours lie on its own device. Each device has exactly 2 blocks with a neighbour on another device in each of +y, -y, +z, -z; those of +y and -z lie on the device numbered one higher, those of -y and +z on the device numbered one lower (both counted around the last device back to device 0). `new_owner`: an occupied block stays on its device or goes to the device numbered one lower or one higher; a device hands at most 1 block to each side, and in every draw some device hands 1 to a side and some device receives 1 from both sides. Blocks keep their order along the curve. -1 exactly for empty slots. `new_slot`: on every device the new slots of the blocks it receives or keeps are distinct and fill 0 up to its new count minus one, at most 8 blocks; some device ends with all 8 slots full. -1 exactly for empty slots.
All inputs are finite; a program needn't handle non-finite values.
Results may differ from a plain program's by a relative error of at most 0.0003.
Values sent between devices are 32-bit elements; how exact they have to be, the bound alone decides.
A program may use at most 256 MiB of HBM per device.

v0:
```python
import functools

import jax
import jax.numpy as jnp
from jax import lax
from jax.experimental import pallas as pl
from jax.experimental.pallas import tpu as pltpu
from jax.sharding import PartitionSpec as P

MESH = pl.DeviceIdType.MESH
AXES = ("gx", "gy")
BLOCKS = 8
LANES = 128
PAIRS = 32
SLABS = 8
TOP = 8
ROWS = 80
F32 = jnp.float32


def lanes_of():
    lane = lax.broadcasted_iota(jnp.int32, (8, LANES), 1)
    cell = lane & 63
    return {
        "upper": lane >= 64,
        "odd": (lane & 1) == 1,
        "pair": cell >> 1,
        "last": cell == 63,
        "edge": (cell == 63) | (cell == 0),
    }


def turned(tile, shift):
    shift %= LANES
    return tile if shift == 0 else pltpu.roll(tile, shift, tile.ndim - 1)


def mobility(values):
    square = values - values * values
    return 0.00075 + 0.04 * (square * square)


def slab(xo):
    return pl.ds(pl.multiple_of(TOP + 8 * xo, 8), 8)


def eight(xo):
    return pl.ds(pl.multiple_of(8 * xo, 8), 8)


def first_row(masks, field, scaled, rows):
    z_face = jnp.zeros((8, LANES), F32)
    ends = []
    for yp in range(PAIRS):
        tile = field[yp, rows, :]
        z_face = jnp.where(masks["pair"] == yp, turned(tile, 2 * yp - 63), z_face)
        scaled[yp, rows, :] = mobility(tile)
        if yp in (0, PAIRS - 1):
            ends.append(tile)
    return z_face, jnp.where(masks["upper"], ends[1], ends[0])


def chemical_row(masks, field, chem, rows, base, y_halo, z_halo):
    above, below = pl.ds(base + 1, 8), pl.ds(base - 1, 8)
    z_face = jnp.zeros((8, LANES), F32)
    ends = []
    before = y_halo
    tile = field[0, rows, :]
    swapped = turned(tile, 64)
    for yp in range(PAIRS):
        if yp < PAIRS - 1:
            following = field[yp + 1, rows, :]
            after = turned(following, 64)
        else:
            following, after = None, y_halo
        total = field[yp, above, :] + field[yp, below, :]
        total = total + (swapped + jnp.where(masks["upper"], after, before))
        side = turned(z_halo, 63 - 2 * yp)
        high = jnp.where(masks["last"], side, turned(tile, -1))
        low = jnp.where(masks["edge"] & ~masks["last"], side, turned(tile, 1))
        total = total + (high + low)
        value = tile * (14.0 + tile * (4.0 * tile - 6.0)) - (total + total)
        chem[yp, rows, :] = value
        z_face = jnp.where(masks["pair"] == yp, turned(value, 2 * yp - 63), z_face)
        if yp in (0, PAIRS - 1):
            ends.append(value)
        before, tile, swapped = swapped, following, after
    return z_face, jnp.where(masks["upper"], ends[1], ends[0])


def advance_row(masks, field, chem, scaled, out, rows, out_rows, base, layers, faces):
    field_y, field_z, chem_y, chem_z = layers
    field_face, chem_face = faces
    above, below = pl.ds(base + 1, 8), pl.ds(base - 1, 8)
    side_flux = (mobility(field_face) + mobility(field_z)) * (chem_z - chem_face)
    u_before, m_before = chem_y, mobility(field_y)
    u_halo, m_halo = u_before, m_before
    u, m = chem[0, rows, :], scaled[0, rows, :]
    u_swapped, m_swapped = turned(u, 64), turned(m, 64)
    for yp in range(PAIRS):
        if yp < PAIRS - 1:
            u_next, m_next = chem[yp + 1, rows, :], scaled[yp + 1, rows, :]
            u_after, m_after = turned(u_next, 64), turned(m_next, 64)
        else:
            u_next = m_next = None
            u_after, m_after = u_halo, m_halo
        flux = (m + scaled[yp, above, :]) * (chem[yp, above, :] - u)
        flux = flux + (m + scaled[yp, below, :]) * (chem[yp, below, :] - u)
        flux = flux + (m + m_swapped) * (u_swapped - u)
        u_far = jnp.where(masks["upper"], u_after, u_before)
        m_far = jnp.where(masks["upper"], m_after, m_before)
        flux = flux + (m + m_far) * (u_far - u)
        along = (m + turned(m, -1)) * (turned(u, -1) - u)
        along = jnp.where(masks["last"], 0.0, along)
        outer = jnp.where(masks["edge"], turned(side_flux, 63 - 2 * yp), 0.0)
        flux = flux + (along - turned(along, 1) + outer)
        out[yp, out_rows, :] = field[yp, rows, :] + flux
        u_before, m_before = u_swapped, m_swapped
        u, m, u_swapped, m_swapped = u_next, m_next, u_after, m_after


def place():
    size = lax.axis_size(AXES)
    minor = lax.axis_size("gy")
    me = lax.axis_index("gx") * minor + lax.axis_index("gy")
    upper, lower = lax.rem(me + 1, size), lax.rem(me + size - 1, size)

    def coordinates(device):
        return (device // minor, lax.rem(device, minor))

    return me, coordinates(upper), coordinates(lower)


def remote(source, target, send, receive, device):
    return pltpu.make_async_remote_copy(
        source, target, send, receive, device_id=device, device_id_type=MESH
    )


def own_kernel(
    c_hbm, links, owner, slot, field, got, got_layers, got_marks,
    scaled, chem, right, y_c, z_c, y_u, z_u, sent_c, sent_u, came_c, came_u, packed, marks, table,
    load_sem, face_send, face_recv, block_send, block_recv, pack_send, pack_recv,
):
    me, upper, lower = place()
    masks = lanes_of()
    full = {
        "upper": lax.broadcasted_iota(jnp.int32, (64, LANES), 1) >= 64,
        "odd": (lax.broadcasted_iota(jnp.int32, (64, LANES), 1) & 1) == 1,
    }

    def load(b, xo):
        return pltpu.make_async_copy(c_hbm.at[b, xo], field.at[b, :, slab(xo), :], load_sem.at[b, xo])

    @pl.loop(0, BLOCKS * SLABS)
    def _(i):
        load(i // SLABS, i % SLABS).start()

    barrier = pltpu.get_barrier_semaphore()
    for device in (upper, lower):
        pl.semaphore_signal(barrier, inc=1, device_id=device, device_id_type=MESH)

    def link(b, d):
        return links[b * 6 + d]

    def scan(d):
        least, first, second = jnp.int32(BLOCKS), jnp.int32(BLOCKS - 1), jnp.int32(0)
        for b in range(BLOCKS):
            p = link(b, d)
            far = (p >= 0) & ((p >> 3) != me)
            least = jnp.where(far, jnp.minimum(least, p & 7), least)
            first = jnp.where(far, jnp.minimum(first, b), first)
            second = jnp.where(far, b, second)
        return least, first, second

    near_base = {2: 8, 3: 8, 4: 8, 5: 16}
    far_base = {2: 18, 3: 16, 4: 24, 5: 26}
    picks = {}
    for d in (2, 3, 4, 5):
        least, first, second = scan(d)
        picks[d] = (first, second)
        for b in range(BLOCKS):
            p = link(b, d)
            part = p & 7
            far = far_base[d] + (part > least).astype(jnp.int32)
            near = jnp.where((p >> 3) == me, near_base[d] + part, far)
            table[b * 6 + d] = jnp.where(p < 0, b, near)
    moving, mark_right, mark_left = jnp.int32(0), jnp.int32(0), jnp.int32(0)
    for b in range(BLOCKS):
        goes_right, goes_left = owner[b] == me + 1, owner[b] == me - 1
        moving = jnp.where(goes_right, b, moving)
        mark_right = jnp.where(goes_right, slot[b] + 1, mark_right)
        mark_left = jnp.where((owner[b] >= 0) & goes_left, slot[b] + 1, mark_left)
    marks[0] = jnp.full((8, LANES), mark_right, jnp.int32).astype(F32)
    marks[1] = jnp.full((8, LANES), mark_left, jnp.int32).astype(F32)

    def keep_faces(y_table, z_table, b, xo, y_face, z_face):
        part = eight(xo)
        y_table[b, part, :] = y_face
        y_table[BLOCKS + b, part, :] = turned(y_face, 64)
        z_table[b, part, :] = z_face
        z_table[BLOCKS + b, part, :] = turned(z_face, 63)
        z_table[2 * BLOCKS + b, part, :] = turned(z_face, 65)

    @pl.loop(0, BLOCKS * SLABS)
    def _(i):
        load(i // SLABS, i % SLABS).wait()

    @pl.loop(0, BLOCKS * SLABS)
    def _(i):
        b, xo = i // SLABS, i % SLABS
        z_face, y_face = first_row(masks, field.at[b], scaled.at[b], slab(xo))
        keep_faces(y_c, z_c, b, xo, y_face, z_face)

    pl.semaphore_wait(barrier, 2)

    def fill(message, y_table, z_table):
        message[0, 0] = jnp.where(
            full["upper"], y_table[picks[2][0]], turned(y_table[picks[2][1]], 64)
        )
        message[0, 1] = jnp.where(
            full["odd"], z_table[picks[5][0]], turned(z_table[picks[5][1]], -1)
        )
        message[1, 0] = jnp.where(
            full["upper"], turned(y_table[picks[3][1]], 64), y_table[picks[3][0]]
        )
        message[1, 1] = jnp.where(
            full["odd"], turned(z_table[picks[4][1]], 1), z_table[picks[4][0]]
        )

    def face_copies(k, message, came):
        return [
            remote(message.at[side], came.at[side], face_send.at[k, side], face_recv.at[k, side], device)
            for side, device in enumerate((upper, lower))
        ]

    def take(came, y_table, z_table):
        low_y, low_z, high_y, high_z = came[0, 0], came[0, 1], came[1, 0], came[1, 1]
        y_table[16], y_table[17] = turned(low_y, 64), low_y
        y_table[18], y_table[19] = turned(high_y, 64), high_y
        z_table[24], z_table[25] = turned(low_z, 63), turned(low_z, 64)
        z_table[26], z_table[27] = turned(high_z, 65), turned(high_z, 64)

    def outside(y_table, z_table, b, part):
        y_layer = jnp.where(
            masks["upper"] if part is not None else full["upper"],
            *(
                y_table[table[b * 6 + d], part, :] if part is not None else y_table[table[b * 6 + d]]
                for d in (2, 3)
            ),
        )
        z_up, z_down = (
            z_table[table[b * 6 + d], part, :] if part is not None else z_table[table[b * 6 + d]]
            for d in (4, 5)
        )
        return y_layer, jnp.where(masks["odd"] if part is not None else full["odd"], z_down, z_up)

    def x_layers(values, b):
        high, low = link(b, 0), link(b, 1)
        high_block = jnp.where(high < 0, b, high & 7)
        low_block = jnp.where(low < 0, b, low & 7)
        from_low = jnp.where(low < 0, values[b, :, 8:9, :], values[low_block, :, 71:72, :])
        from_high = jnp.where(high < 0, values[b, :, 71:72, :], values[high_block, :, 8:9, :])
        return from_low, from_high

    fill(sent_c, y_c, z_c)
    first_faces = face_copies(0, sent_c, came_c)
    for copy in first_faces:
        copy.start()

    @pl.loop(0, SLABS)
    def _(xo):
        for yp in range(PAIRS):
            right[xo, yp] = field[moving, yp, slab(xo), :]

    def block_copies(xo):
        target = slab(xo)
        return [
            remote(right.at[xo], got.at[0, :, target, :], block_send.at[0, xo], block_recv.at[0, xo], upper),
            remote(c_hbm.at[0, xo], got.at[1, :, target, :], block_send.at[1, xo], block_recv.at[1, xo], lower),
        ]

    early = 3
    for xo in range(early):
        for copy in block_copies(xo):
            copy.start()

    @pl.loop(0, BLOCKS)
    def _(b):
        from_low, from_high = x_layers(field, b)
        field[b, :, 7:8, :] = from_low
        field[b, :, 72:73, :] = from_high
        scaled[b, :, 7:8, :] = mobility(from_low)
        scaled[b, :, 72:73, :] = mobility(from_high)

    for copy in first_faces:
        copy.wait_recv()
    take(came_c, y_c, z_c)

    @pl.loop(0, BLOCKS * SLABS)
    def _(i):
        b, xo = i // SLABS, i % SLABS
        y_halo, z_halo = outside(y_c, z_c, b, eight(xo))
        z_face, y_face = chemical_row(
            masks, field.at[b], chem.at[b], slab(xo), TOP + 8 * xo, y_halo, z_halo
        )
        keep_faces(y_u, z_u, b, xo, y_face, z_face)

    fill(sent_u, y_u, z_u)
    second_faces = face_copies(1, sent_u, came_u)
    for copy in second_faces:
        copy.start()
    for xo in range(early, SLABS):
        for copy in block_copies(xo):
            copy.start()

    @pl.loop(0, BLOCKS)
    def _(b):
        from_low, from_high = x_layers(chem, b)
        chem[b, :, 7:8, :] = from_low
        chem[b, :, 72:73, :] = from_high

    def pack(k, values, y_table, z_table):
        for side, b in ((0, moving), (1, 0)):
            y_layer, z_layer = outside(y_table, z_table, b, None)
            packed[side, k, 0] = y_layer
            packed[side, k, 1] = z_layer
            for yp in range(PAIRS):
                packed[side, k, 2, yp : yp + 1, :] = values[b, yp, 7:8, :]
                packed[side, k, 2, PAIRS + yp : PAIRS + yp + 1, :] = values[b, yp, 72:73, :]

    pack(0, field, y_c, z_c)
    for copy in second_faces:
        copy.wait_recv()
    take(came_u, y_u, z_u)
    pack(1, chem, y_u, z_u)
    pack_copies = []
    for side, device in enumerate((upper, lower)):
        pack_copies.append(
            remote(packed.at[side], got_layers.at[side], pack_send.at[0, side], pack_recv.at[0, side], device)
        )
        pack_copies.append(
            remote(marks.at[side], got_marks.at[side], pack_send.at[1, side], pack_recv.at[1, side], device)
        )
    for copy in pack_copies:
        copy.start()

    @pl.loop(0, BLOCKS * SLABS)
    def _(i):
        b, xo = i // SLABS, i % SLABS
        part = eight(xo)
        layers = outside(y_c, z_c, b, part) + outside(y_u, z_u, b, part)
        faces = (z_c[b, part, :], z_u[b, part, :])
        rows = slab(xo)
        advance_row(
            masks, field.at[b], chem.at[b], scaled.at[b], field.at[b], rows, rows, TOP + 8 * xo, layers, faces
        )

    for copy in pack_copies:
        copy.wait()
    for xo in range(SLABS):
        for copy in block_copies(xo):
            copy.wait()
    for copy in first_faces + second_faces:
        copy.wait_send()


def layout_kernel(
    field, got, got_layers, got_marks, owner, slot, out,
    arrived, scaled, chem, stepped, zeros, z_c, z_u, keep_sem, zero_sem, new_sem,
):
    me, _, _ = place()
    masks = lanes_of()
    kept = jnp.int32(0)
    for b in range(BLOCKS):
        stays = owner[b] == me
        kept = kept + stays.astype(jnp.int32)

        @pl.when(stays)
        def _(b=b):
            for xo in range(SLABS):
                pltpu.make_async_copy(
                    field.at[b, :, pl.ds(TOP + 8 * xo, 8), :], out.at[slot[b], xo], keep_sem.at[b, xo]
                ).start()

    places = [jnp.max(got_marks[side]).astype(jnp.int32) for side in range(2)]
    count = kept
    for target in places:
        count = count + (target > 0).astype(jnp.int32)
    zeros[...] = jnp.zeros_like(zeros)
    for s in range(BLOCKS):

        @pl.when(s >= count)
        def _(s=s):
            pltpu.make_async_copy(zeros, out.at[s], zero_sem.at[s]).start()

    for side in range(2):

        @pl.when(places[side] > 0)
        def _(side=side):
            layers = got_layers.at[side]

            @pl.loop(0, SLABS)
            def _(xo):
                rows = slab(xo)
                for yp in range(PAIRS):
                    arrived[yp, rows, :] = got[side, yp, rows, :]
                z_face, _ = first_row(masks, arrived, scaled, rows)
                z_c[eight(xo), :] = z_face

            for yp in range(PAIRS):
                for k, values in ((0, arrived), (1, chem)):
                    values[yp, 7:8, :] = layers[k, 2, yp : yp + 1, :]
                    values[yp, 72:73, :] = layers[k, 2, PAIRS + yp : PAIRS + yp + 1, :]
                scaled[yp, 7:8, :] = mobility(layers[0, 2, yp : yp + 1, :])
                scaled[yp, 72:73, :] = mobility(layers[0, 2, PAIRS + yp : PAIRS + yp + 1, :])

            @pl.loop(0, SLABS)
            def _(xo):
                part = eight(xo)
                z_face, _ = chemical_row(
                    masks, arrived, chem, slab(xo), TOP + 8 * xo, layers[0, 0, part, :], layers[0, 1, part, :]
                )
                z_u[part, :] = z_face

            @pl.loop(0, SLABS)
            def _(xo):
                part = eight(xo)
                around = (layers[0, 0, part, :], layers[0, 1, part, :], layers[1, 0, part, :], layers[1, 1, part, :])
                advance_row(
                    masks, arrived, chem, scaled, stepped.at[side, xo], slab(xo), pl.ds(0, 8), TOP + 8 * xo,
                    around, (z_c[part, :], z_u[part, :]),
                )

            pltpu.make_async_copy(stepped.at[side], out.at[places[side] - 1], new_sem.at[side]).start()

    for b in range(BLOCKS):

        @pl.when(owner[b] == me)
        def _(b=b):
            for xo in range(SLABS):
                pltpu.make_async_copy(
                    field.at[b, :, pl.ds(TOP + 8 * xo, 8), :], out.at[slot[b], xo], keep_sem.at[b, xo]
                ).wait()

    for s in range(BLOCKS):

        @pl.when(s >= count)
        def _(s=s):
            pltpu.make_async_copy(zeros, out.at[s], zero_sem.at[s]).wait()

    for side in range(2):

        @pl.when(places[side] > 0)
        def _(side=side):
            pltpu.make_async_copy(stepped.at[side], out.at[places[side] - 1], new_sem.at[side]).wait()


def per_device(concentration, neighbour, new_owner, new_slot):
    tiles = concentration.reshape(BLOCKS, SLABS, 8, PAIRS, LANES).transpose(0, 1, 3, 2, 4)
    links = neighbour.reshape(BLOCKS * 6)
    anywhere = pl.BlockSpec(memory_space=pl.ANY)
    scalars = pl.BlockSpec(memory_space=pltpu.SMEM)
    vector = pl.BlockSpec(memory_space=pltpu.VMEM)
    padded = (PAIRS, ROWS, LANES)
    face = (64, LANES)
    tables = [pltpu.VMEM((20, *face), F32), pltpu.VMEM((28, *face), F32)]
    dma = pltpu.SemaphoreType.DMA
    field, got, got_layers, got_marks = pl.pallas_call(
        own_kernel,
        out_shape=[
            pltpu.VMEM((BLOCKS, *padded), F32),
            pltpu.VMEM((2, *padded), F32),
            pltpu.VMEM((2, 2, 3, *face), F32),
            pltpu.VMEM((2, 8, LANES), F32),
        ],
        in_specs=[anywhere, scalars, scalars, scalars],
        out_specs=[vector] * 4,
        scratch_shapes=[
            pltpu.VMEM((BLOCKS, *padded), F32),
            pltpu.VMEM((BLOCKS, *padded), F32),
            pltpu.VMEM((SLABS, PAIRS, 8, LANES), F32),
            *tables,
            *tables,
            *[pltpu.VMEM((2, 2, *face), F32)] * 4,
            pltpu.VMEM((2, 2, 3, *face), F32),
            pltpu.VMEM((2, 8, LANES), F32),
            pltpu.SMEM((BLOCKS * 6,), jnp.int32),
            dma((BLOCKS, SLABS)),
            dma((2, 2)),
            dma((2, 2)),
            dma((2, SLABS)),
            dma((2, SLABS)),
            dma((2, 2)),
            dma((2, 2)),
        ],
        compiler_params=pltpu.CompilerParams(
            collective_id=0, has_side_effects=True, vmem_limit_bytes=48 << 20
        ),
    )(tiles, links, new_owner, new_slot)
    out = pl.pallas_call(
        layout_kernel,
        out_shape=jax.ShapeDtypeStruct((BLOCKS, SLABS, PAIRS, 8, LANES), F32),
        in_specs=[vector] * 4 + [scalars] * 2,
        out_specs=anywhere,
        scratch_shapes=[
            pltpu.VMEM(padded, F32),
            pltpu.VMEM(padded, F32),
            pltpu.VMEM(padded, F32),
            pltpu.VMEM((2, SLABS, PAIRS, 8, LANES), F32),
            pltpu.VMEM((SLABS, PAIRS, 8, LANES), F32),
            pltpu.VMEM(face, F32),
            pltpu.VMEM(face, F32),
            dma((BLOCKS, SLABS)),
            dma((BLOCKS,)),
            dma((2,)),
        ],
        compiler_params=pltpu.CompilerParams(vmem_limit_bytes=40 << 20),
    )(field, got, got_layers, got_marks, new_owner, new_slot)
    return out.transpose(0, 1, 3, 2, 4).reshape(concentration.shape)


def solution(mesh):
    return jax.shard_map(
        per_device,
        mesh=mesh,
        in_specs=(P(AXES, None, None), P(AXES, None), P(AXES), P(AXES)),
        out_specs=P(AXES, None, None),
        check_vma=False,
    )
```

profile of v0, /device:TPU:65, one launch (start us, length us, event | category | flops | bytes accessed | tf_op | source)
XLA Modules:
  0.0 139.7 jit_solution(10306798351530318833)
XLA Ops:
  0.0 0.0 copy-start.3
  0.0 0.0 copy-start.2
  0.0 1.3 reshape.10.links
  1.3 103.7 %shard_map.46 = (f32[8,32,80,128]{3,2,1,0:T(8,128)S(1)}, f32[2,32,80,128]{3,2,1,0:T(8,128)S(1)}, f32[2,2,3,64,128]{4,3,2,1,0:T(8,128)S(1)}, f32[2,8,128]{2,1,0:T(8,128)S(1)}) custom-call(f32[8,8,32,8,128]{4,3,2,1,0:T(8,128)} %bitcast.6, s32[48]{0:T(128)} %reshape.10.links, s32[8]{0:T(128)} %owner.3, s32[8]{0:T(128)} %slot.3), custom_call_target="tpu_custom_call" | custom-call | tf_op jit(solution)/shard_map/pallas_call | solution.py:469
  105.0 0.0 copy-start
  105.0 4.0 %copy-done = f32[8,32,80,128]{3,2,1,0:T(8,128)} copy-done((f32[8,32,80,128]{3,2,1,0:T(8,128)}, f32[8,32,80,128]{3,2,1,0:T(8,128)S(1)}, u32[]{:S(2)}) %copy-start) | copy-done | bytes 10485784
  108.9 0.0 copy-done.3
  108.9 0.0 copy-done.2
  108.9 0.0 copy-start.1
  108.9 4.0 %copy-done.1 = f32[8,32,80,128]{3,2,1,0:T(8,128)S(1)} copy-done((f32[8,32,80,128]{3,2,1,0:T(8,128)S(1)}, f32[8,32,80,128]{3,2,1,0:T(8,128)}, u32[]{:S(2)}) %copy-start.1) | copy-done | bytes 10485784
  112.9 26.8 %shard_map.47 = f32[8,8,32,8,128]{4,3,2,1,0:T(8,128)} custom-call(f32[8,32,80,128]{3,2,1,0:T(8,128)S(1)} %copy-done.1, f32[2,32,80,128]{3,2,1,0:T(8,128)S(1)} %get-tuple-element.10.got, f32[2,2,3,64,128]{4,3,2,1,0:T(8,128)S(1)} %get-tuple-element.11.got_layers, f32[2,8,128]{2,1,0:T(8,128)S(1)} %get-tuple-element.12.got_marks, s32[8]{0:T(128)S(1)} %copy-done.2, ...), custom_call_target="tpu_custom_call" | custom-call | tf_op jit(solution)/shard_map/pallas_call | solution.py:501
Async XLA Ops:
  0.0 108.9 %copy-start.3 = (s32[8]{0:T(128)S(1)}, s32[8]{0:T(128)}, u32[]{:S(2)}) copy-start(s32[8]{0:T(128)} %slot.3) | copy-start | bytes 100
  0.0 108.9 %copy-start.2 = (s32[8]{0:T(128)S(1)}, s32[8]{0:T(128)}, u32[]{:S(2)}) copy-start(s32[8]{0:T(128)} %owner.3) | copy-start | bytes 100
  105.0 4.0 %copy-start = (f32[8,32,80,128]{3,2,1,0:T(8,128)}, f32[8,32,80,128]{3,2,1,0:T(8,128)S(1)}, u32[]{:S(2)}) copy-start(f32[8,32,80,128]{3,2,1,0:T(8,128)S(1)} %get-tuple-element.9.field) | copy-start | bytes 31457284
  108.9 4.0 %copy-start.1 = (f32[8,32,80,128]{3,2,1,0:T(8,128)S(1)}, f32[8,32,80,128]{3,2,1,0:T(8,128)}, u32[]{:S(2)}) copy-start(f32[8,32,80,128]{3,2,1,0:T(8,128)} %copy-done) | copy-start | bytes 31457284
where the time goes:
time: 141 us; the launch traced here: 140 us
  Pallas kernels  130 us (92%)
  local copies, waits for them, and re-layouts  9.25 us (7%)
    pallas_call x1, Pallas kernels, per_device(): pl.pallas_call(own_kernel, out_shape=[pltpu.VMEM((BLOCKS, *padded), F32),...  104 us
    pallas_call x1, Pallas kernels, per_device(): pl.pallas_call(layout_kernel, out_shape=jax.ShapeDtypeStruct((BLOCKS, SLA...  26.8 us
    unnamed x8, local copies, waits for them, and re-layouts  7.94 us

commit v1 on v0

v1 whole, which is shorter than its diff:
```python
import jax
import jax.numpy as jnp
from jax import lax
from jax.experimental import pallas as pl
from jax.experimental.pallas import tpu as pltpu
from jax.sharding import PartitionSpec as P

MESH = pl.DeviceIdType.MESH
AXES = ("gx", "gy")
BLOCKS = 8
LANES = 128
TILES = 32
SLABS = 8
TOP = 8
PITCH = 80
F32 = jnp.float32
FACE = (32, LANES)


def masks_of():
    lane = lax.broadcasted_iota(jnp.int32, (8, LANES), 1)
    xc, yc = lane & 15, lane >> 4
    return {
        "xc": xc,
        "yc": yc,
        "x_first": xc == 0,
        "x_last": xc == 15,
        "y_first": yc == 0,
        "y_last": yc == 7,
    }


def turned(tile, shift):
    if isinstance(shift, int):
        shift %= LANES
        if shift == 0:
            return tile
    return pltpu.roll(tile, shift, 1)


def mobility(values):
    square = values - values * values
    return 0.00075 + 0.04 * (square * square)


def slab(z, offset=0):
    if offset:
        return pl.ds(TOP + 8 * z + offset, 8)
    return pl.ds(pl.multiple_of(TOP + 8 * z, 8), 8)


def eight(z):
    return pl.ds(pl.multiple_of(8 * z, 8), 8)


def part(k):
    return pl.ds(8 * k, 8)


def rows_of(block):
    return block.reshape(TILES * PITCH, LANES)


def z_rows(block, row):
    return rows_of(block)[pl.ds(row, TILES, stride=PITCH), :]


def set_z_rows(block, row, values):
    rows_of(block)[pl.ds(row, TILES, stride=PITCH), :] = values


def shifted_sides(masks, block, z, halo):
    rows = slab(z)
    sides = []
    for yf in range(8):
        own = turned(block[yf, rows, :], -1)
        sides.append(jnp.where(masks["x_last"], halo(0, yf), own))
    for yf in range(8):
        own = turned(block[24 + yf, rows, :], 1)
        sides.append(jnp.where(masks["x_first"], halo(1, yf), own))
    for xf in range(4):
        own = turned(block[8 * xf, rows, :], -16)
        sides.append(jnp.where(masks["y_last"], halo(2, xf), own))
    for xf in range(4):
        own = turned(block[8 * xf + 7, rows, :], 16)
        sides.append(jnp.where(masks["y_first"], halo(3, xf), own))
    return sides


def near(block, z, sides, xf, yf):
    rows, tile = slab(z), 8 * xf + yf
    return (
        block[tile + 8, rows, :] if xf < 3 else sides[yf],
        block[tile - 8, rows, :] if xf > 0 else sides[8 + yf],
        block[tile + 1, rows, :] if yf < 7 else sides[16 + xf],
        block[tile - 1, rows, :] if yf > 0 else sides[20 + xf],
        block[tile, slab(z, 1), :],
        block[tile, slab(z, -1), :],
    )


def chemical_slab(masks, field, chem, side_mobility, z, halo, keep):
    sides = shifted_sides(masks, field, z, halo)
    for k, values in enumerate(sides):
        side_mobility[k, eight(z), :] = mobility(values)
    rows = slab(z)
    for xf in range(4):
        for yf in range(8):
            tile = field[8 * xf + yf, rows, :]
            a, b, c, d, e, f = near(field, z, sides, xf, yf)
            total = ((a + b) + (c + d)) + (e + f)
            value = tile * (14.0 + tile * (4.0 * tile - 6.0)) - (total + total)
            chem[8 * xf + yf, rows, :] = value
            if keep is not None and yf in (0, 7):
                keep(xf, yf, value)


def advance_slab(masks, field, chem, scaled, side_mobility, out, z, halo):
    sides = shifted_sides(masks, chem, z, halo)
    side_scaled = [side_mobility[k, eight(z), :] for k in range(24)]
    rows = slab(z)
    for xf in range(4):
        for yf in range(8):
            tile = 8 * xf + yf
            u, m = chem[tile, rows, :], scaled[tile, rows, :]
            flux = None
            for u_near, m_near in zip(near(chem, z, sides, xf, yf), near(scaled, z, side_scaled, xf, yf)):
                term = (m + m_near) * (u_near - u)
                flux = term if flux is None else flux + term
            out[tile, rows, :] = field[tile, rows, :] + flux


def y_part(masks, tile, yf, z, held):
    shift = lax.rem((z - (7 if yf else 0)) * 16 + LANES, LANES)
    return jnp.where(masks["yc"] == z, turned(tile, shift), held)


def y_halo(face, side, xf, z):
    place = 7 if side == 2 else 0
    return turned(face[part(xf), :], lax.rem((place - z) * 16 + LANES, LANES))


def x_halo(face, side, yf, z):
    place = 15 if side == 0 else 0
    spot = (yf & 1) * 8 + z
    return turned(face[part(yf >> 1), :], lax.rem(place - spot + LANES, LANES))


def group_in(stage, xf, pair):
    rows = [stage[4 * yc + pair, pl.ds(xf, 16, stride=4), :] for yc in range(8)]
    return jnp.concatenate(rows, 0).T


def group_out(stage, xf, pair, block):
    tile = 8 * xf + 2 * pair
    both = jnp.concatenate([block[tile, TOP : TOP + 64, :], block[tile + 1, TOP : TOP + 64, :]], 0).T
    for yc in range(8):
        stage[4 * yc + pair, pl.ds(xf, 16, stride=4), :] = both[16 * yc : 16 * yc + 16]


def place():
    size = lax.axis_size(AXES)
    minor = lax.axis_size("gy")
    me = lax.axis_index("gx") * minor + lax.axis_index("gy")
    upper, lower = lax.rem(me + 1, size), lax.rem(me + size - 1, size)

    def coordinates(device):
        return (device // minor, lax.rem(device, minor))

    return me, coordinates(upper), coordinates(lower)


def remote(source, target, send, receive, device):
    return pltpu.make_async_remote_copy(
        source, target, send, receive, device_id=device, device_id_type=MESH
    )


def own_kernel(
    c_hbm, links, owner, slot, stage, got, got_layers, got_marks,
    field, chem, scaled, side_mobility, pay, y_c, z_c, y_u, z_u, sent_c, sent_u, came_c, came_u, packed, marks, table,
    load_sem, face_send, face_recv, block_send, block_recv, pack_send, pack_recv,
):
    me, upper, lower = place()
    masks = masks_of()

    def load(b, xo):
        return pltpu.make_async_copy(c_hbm.at[b, xo], stage.at[b, :, eight(xo), :], load_sem.at[b, xo])

    @pl.loop(0, BLOCKS * SLABS)
    def _(i):
        load(i // SLABS, i % SLABS).start()

    barrier = pltpu.get_barrier_semaphore()
    for device in (upper, lower):
        pl.semaphore_signal(barrier, inc=1, device_id=device, device_id_type=MESH)

    def link(b, d):
        return links[b * 6 + d]

    near_base = {2: 0, 3: 8, 4: 0, 5: 8}
    far_base = {2: 18, 3: 16, 4: 16, 5: 18}
    own_base = {2: 8, 3: 0, 4: 8, 5: 0}
    picks = {}
    for d in (2, 3, 4, 5):
        least, first, second = jnp.int32(BLOCKS), jnp.int32(BLOCKS - 1), jnp.int32(0)
        for b in range(BLOCKS):
            p = link(b, d)
            far = (p >= 0) & ((p >> 3) != me)
            least = jnp.where(far, jnp.minimum(least, p & 7), least)
            first = jnp.where(far, jnp.minimum(first, b), first)
            second = jnp.where(far, b, second)
        picks[d] = (first + own_base[d], second + own_base[d])
        for b in range(BLOCKS):
            p = link(b, d)
            far = far_base[d] + ((p & 7) > least).astype(jnp.int32)
            index = jnp.where((p >> 3) == me, near_base[d] + (p & 7), far)
            table[b * 6 + d] = jnp.where(p < 0, own_base[d] + b, index)
    moving, mark_right, mark_left = jnp.int32(0), jnp.int32(0), jnp.int32(0)
    for b in range(BLOCKS):
        goes_right, goes_left = owner[b] == me + 1, owner[b] == me - 1
        moving = jnp.where(goes_right, b, moving)
        mark_right = jnp.where(goes_right, slot[b] + 1, mark_right)
        mark_left = jnp.where((owner[b] >= 0) & goes_left, slot[b] + 1, mark_left)
    marks[0] = jnp.full((8, LANES), mark_right, jnp.int32).astype(F32)
    marks[1] = jnp.full((8, LANES), mark_left, jnp.int32).astype(F32)

    def take_in(b, xf, pair, extra=None):
        both = group_in(stage.at[b], xf, pair)
        for h in range(2):
            tile, values = 8 * xf + 2 * pair + h, both[64 * h : 64 * h + 64]
            if extra is None:
                field[b, tile, TOP : TOP + 64, :] = values
                scaled[b, tile, TOP : TOP + 64, :] = mobility(values)
            else:
                pay[extra, tile] = values

    @pl.loop(0, BLOCKS)
    def _(b):
        for xo in range(SLABS):
            load(b, xo).wait()

        @pl.loop(0, 8)
        def _(k):
            for q in range(2):
                take_in(b, k // 2, (k % 2) * 2 + q)

    @pl.loop(0, 8)
    def _(k):
        for q in range(2):
            take_in(moving, k // 2, (k % 2) * 2 + q, 0)

    @pl.loop(0, TILES)
    def _(t):
        pay[1, t] = field[0, t, TOP : TOP + 64, :]

    def z_faces(values, z_table):
        @pl.loop(0, BLOCKS)
        def _(b):
            z_table[b] = z_rows(values.at[b], TOP)
            z_table[BLOCKS + b] = z_rows(values.at[b], TOP + 63)

    z_faces(field, z_c)

    def keep_y(y_table, b, z):
        def keep(xf, yf, value):
            entry = BLOCKS + b if yf else b
            y_table[entry, part(xf), :] = y_part(masks, value, yf, z, y_table[entry, part(xf), :])

        return keep

    @pl.loop(0, BLOCKS * SLABS)
    def _(i):
        b, z = i // SLABS, i % SLABS
        keep = keep_y(y_c, b, z)
        for xf in range(4):
            for yf in (0, 7):
                keep(xf, yf, field[b, 8 * xf + yf, slab(z), :])

    pl.semaphore_wait(barrier, 2)

    def fill(message, y_table, z_table):
        for side, (y_dir, z_dir) in enumerate(((2, 5), (3, 4))):
            for k in range(2):
                message[side, k] = y_table[picks[y_dir][k]]
                message[side, 2 + k] = z_table[picks[z_dir][k]]

    def face_copies(k, message, came):
        return [
            remote(message.at[side], came.at[side], face_send.at[k, side], face_recv.at[k, side], device)
            for side, device in enumerate((upper, lower))
        ]

    def take(came, y_table, z_table):
        for side in range(2):
            for k in range(2):
                y_table[16 + 2 * side + k] = came[side, k]
                z_table[16 + 2 * side + k] = came[side, 2 + k]

    def block_copies(z):
        return [
            remote(
                pay.at[side, :, eight(z), :], got.at[side, :, slab(z), :],
                block_send.at[side, z], block_recv.at[side, z], device,
            )
            for side, device in enumerate((upper, lower))
        ]

    def halo_of(values, y_table, b, z):
        rows = slab(z)
        open_high, open_low = link(b, 0) < 0, link(b, 1) < 0
        high = jnp.where(open_high, b, link(b, 0) & 7)
        low = jnp.where(open_low, b, link(b, 1) & 7)

        def halo(side, k):
            if side == 0:
                return jnp.where(open_high, values[b, 24 + k, rows, :], turned(values[high, k, rows, :], 15))
            if side == 1:
                return jnp.where(open_low, values[b, k, rows, :], turned(values[low, 24 + k, rows, :], -15))
            return y_halo(y_table.at[table[b * 6 + side]], side, k, z)

        return halo

    def set_z(values, z_table, b, scale=None):
        for row, d in ((TOP + 64, 4), (TOP - 1, 5)):
            layer = z_table[table[b * 6 + d]]
            set_z_rows(values.at[b], row, layer)
            if scale is not None:
                set_z_rows(scale.at[b], row, mobility(layer))

    fill(sent_c, y_c, z_c)
    first_faces = face_copies(0, sent_c, came_c)
    for copy in first_faces:
        copy.start()
    early = 3
    for z in range(early):
        for copy in block_copies(z):
            copy.start()
    for copy in first_faces:
        copy.wait_recv()
    take(came_c, y_c, z_c)

    @pl.loop(0, BLOCKS)
    def _(b):
        set_z(field, z_c, b, scaled)

    @pl.loop(0, BLOCKS * SLABS)
    def _(i):
        b, z = i // SLABS, i % SLABS
        chemical_slab(
            masks, field.at[b], chem.at[b], side_mobility.at[b], z, halo_of(field, y_c, b, z), keep_y(y_u, b, z)
        )

    z_faces(chem, z_u)
    fill(sent_u, y_u, z_u)
    second_faces = face_copies(1, sent_u, came_u)
    for copy in second_faces:
        copy.start()
    for z in range(early, SLABS):
        for copy in block_copies(z):
            copy.start()

    def pack(k, values, y_table, z_table):
        for side, b in ((0, moving), (1, 0)):
            for d in (2, 3):
                packed[side, k, d] = y_table[table[b * 6 + d]]
            for d in (4, 5):
                packed[side, k, d] = z_table[table[b * 6 + d]]

            @pl.loop(0, SLABS)
            def _(z, side=side, b=b):
                halo = halo_of(values, y_table, b, z)
                for d in range(2):
                    for yf in range(8):
                        spot = (yf & 1) * 8 + z
                        shift = lax.rem(spot - (0 if d else 15) + LANES, LANES)
                        held = packed[side, k, d, part(yf >> 1), :]
                        packed[side, k, d, part(yf >> 1), :] = jnp.where(
                            masks["xc"] == spot, turned(halo(d, yf), shift), held
                        )

    pack(0, field, y_c, z_c)
    for copy in second_faces:
        copy.wait_recv()
    take(came_u, y_u, z_u)

    @pl.loop(0, BLOCKS)
    def _(b):
        set_z(chem, z_u, b)

    pack(1, chem, y_u, z_u)
    pack_copies = []
    for side, device in enumerate((upper, lower)):
        pack_copies.append(
            remote(packed.at[side], got_layers.at[side], pack_send.at[0, side], pack_recv.at[0, side], device)
        )
        pack_copies.append(
            remote(marks.at[side], got_marks.at[side], pack_send.at[1, side], pack_recv.at[1, side], device)
        )
    for copy in pack_copies:
        copy.start()

    @pl.loop(0, BLOCKS * SLABS)
    def _(i):
        b, z = i // SLABS, i % SLABS
        advance_slab(
            masks, field.at[b], chem.at[b], scaled.at[b], side_mobility.at[b], field.at[b], z,
            halo_of(chem, y_u, b, z),
        )

    @pl.loop(0, BLOCKS * 8)
    def _(i):
        b, k = i // 8, i % 8
        for q in range(2):
            group_out(stage.at[b], k // 2, (k % 2) * 2 + q, field.at[b])

    for copy in pack_copies:
        copy.wait()
    for z in range(SLABS):
        for copy in block_copies(z):
            copy.wait()
    for copy in first_faces + second_faces:
        copy.wait_send()


def layout_kernel(
    stage, got, got_layers, got_marks, owner, slot, out,
    arrived, scaled, chem, stepped, side_mobility, final, zeros, keep_sem, zero_sem, new_sem,
):
    me, _, _ = place()
    masks = masks_of()

    def keep_copy(b, xo):
        return pltpu.make_async_copy(stage.at[b, :, 8 * xo : 8 * xo + 8, :], out.at[slot[b], xo], keep_sem.at[b, xo])

    def new_copy(side, xo):
        return pltpu.make_async_copy(
            final.at[side, :, 8 * xo : 8 * xo + 8, :], out.at[places[side] - 1, xo], new_sem.at[side, xo]
        )

    kept = jnp.int32(0)
    for b in range(BLOCKS):
        stays = owner[b] == me
        kept = kept + stays.astype(jnp.int32)

        @pl.when(stays)
        def _(b=b):
            for xo in range(SLABS):
                keep_copy(b, xo).start()

    places = [jnp.max(got_marks[side]).astype(jnp.int32) for side in range(2)]
    count = kept
    for target in places:
        count = count + (target > 0).astype(jnp.int32)
    zeros[...] = jnp.zeros_like(zeros)
    for s in range(BLOCKS):

        @pl.when(s >= count)
        def _(s=s):
            pltpu.make_async_copy(zeros, out.at[s], zero_sem.at[s]).start()

    for side in range(2):

        @pl.when(places[side] > 0)
        def _(side=side):
            layers = got_layers.at[side]

            def halo_of(k, z):
                def halo(d, f):
                    return (x_halo if d < 2 else y_halo)(layers.at[k, d], d, f, z)

                return halo

            @pl.loop(0, SLABS)
            def _(z):
                rows = slab(z)
                for t in range(TILES):
                    values = got[side, t, rows, :]
                    arrived[t, rows, :] = values
                    scaled[t, rows, :] = mobility(values)

            for row, d in ((TOP + 64, 4), (TOP - 1, 5)):
                set_z_rows(arrived, row, layers[0, d])
                set_z_rows(scaled, row, mobility(layers[0, d]))
                set_z_rows(chem, row, layers[1, d])

            @pl.loop(0, SLABS)
            def _(z):
                chemical_slab(masks, arrived, chem, side_mobility, z, halo_of(0, z), None)

            @pl.loop(0, SLABS)
            def _(z):
                advance_slab(masks, arrived, chem, scaled, side_mobility, stepped, z, halo_of(1, z))

            @pl.loop(0, 8)
            def _(k):
                for q in range(2):
                    group_out(final.at[side], k // 2, (k % 2) * 2 + q, stepped)

            for xo in range(SLABS):
                new_copy(side, xo).start()

    for b in range(BLOCKS):

        @pl.when(owner[b] == me)
        def _(b=b):
            for xo in range(SLABS):
                keep_copy(b, xo).wait()

    for s in range(BLOCKS):

        @pl.when(s >= count)
        def _(s=s):
            pltpu.make_async_copy(zeros, out.at[s], zero_sem.at[s]).wait()

    for side in range(2):

        @pl.when(places[side] > 0)
        def _(side=side):
            for xo in range(SLABS):
                new_copy(side, xo).wait()


def per_device(concentration, neighbour, new_owner, new_slot):
    tiles = concentration.reshape(BLOCKS, SLABS, 8, 32, LANES).transpose(0, 1, 3, 2, 4)
    links = neighbour.reshape(BLOCKS * 6)
    anywhere = pl.BlockSpec(memory_space=pl.ANY)
    scalars = pl.BlockSpec(memory_space=pltpu.SMEM)
    vector = pl.BlockSpec(memory_space=pltpu.VMEM)
    padded = (TILES, PITCH, LANES)
    plain = (TILES, 64, LANES)
    sides = (24, 64, LANES)
    tables = [pltpu.VMEM((20, *FACE), F32)] * 4
    dma = pltpu.SemaphoreType.DMA
    stage, got, got_layers, got_marks = pl.pallas_call(
        own_kernel,
        out_shape=[
            pltpu.VMEM((BLOCKS, *plain), F32),
            pltpu.VMEM((2, *padded), F32),
            pltpu.VMEM((2, 2, 6, *FACE), F32),
            pltpu.VMEM((2, 8, LANES), F32),
        ],
        in_specs=[anywhere, scalars, scalars, scalars],
        out_specs=[vector] * 4,
        scratch_shapes=[
            *[pltpu.VMEM((BLOCKS, *padded), F32)] * 3,
            pltpu.VMEM((BLOCKS, *sides), F32),
            pltpu.VMEM((2, *plain), F32),
            *tables,
            *[pltpu.VMEM((2, 4, *FACE), F32)] * 4,
            pltpu.VMEM((2, 2, 6, *FACE), F32),
            pltpu.VMEM((2, 8, LANES), F32),
            pltpu.SMEM((BLOCKS * 6,), jnp.int32),
            dma((BLOCKS, SLABS)),
            dma((2, 2)),
            dma((2, 2)),
            dma((2, SLABS)),
            dma((2, SLABS)),
            dma((2, 2)),
            dma((2, 2)),
        ],
        compiler_params=pltpu.CompilerParams(
            collective_id=0, has_side_effects=True, vmem_limit_bytes=48 << 20
        ),
    )(tiles, links, new_owner, new_slot)
    out = pl.pallas_call(
        layout_kernel,
        out_shape=jax.ShapeDtypeStruct((BLOCKS, SLABS, 32, 8, LANES), F32),
        in_specs=[vector] * 4 + [scalars] * 2,
        out_specs=anywhere,
        scratch_shapes=[
            *[pltpu.VMEM(padded, F32)] * 4,
            pltpu.VMEM(sides, F32),
            pltpu.VMEM((2, *plain), F32),
            pltpu.VMEM((SLABS, 32, 8, LANES), F32),
            dma((BLOCKS, SLABS)),
            dma((BLOCKS,)),
            dma((2, SLABS)),
        ],
        compiler_params=pltpu.CompilerParams(vmem_limit_bytes=16 << 20),
    )(stage, got, got_layers, got_marks, new_owner, new_slot)
    return out.transpose(0, 1, 3, 2, 4).reshape(concentration.shape)


def solution(mesh):
    return jax.shard_map(
        per_device,
        mesh=mesh,
        in_specs=(P(AXES, None, None), P(AXES, None), P(AXES), P(AXES)),
        out_specs=P(AXES, None, None),
        check_vma=False,
    )
```

time: 141 us -> 70.4 us (0.50)
  Pallas kernels: 130 us -> 68 us
  local copies, waits for them, and re-layouts: 9.25 us -> 1.31 us
    pallas_call x1, Pallas kernels: 104 us -> 59.2 us  [per_device(): pl.pallas_call(own_kernel, out_shape=[pltpu.VMEM((BLOCKS, *plain), F32),...]
    pallas_call x1, Pallas kernels: 26.8 us -> 8.73 us  [per_device(): pl.pallas_call(layout_kernel, out_shape=jax.ShapeDtypeStruct((BLOCKS, SLA...]
    unnamed x8 -> x4, local copies, waits for them, and re-layouts: 7.94 us -> 0.01 us
where the time goes in v1:
time: 70.4 us; the launch traced here: 69.3 us
  Pallas kernels  68 us (97%)
  local copies, waits for them, and re-layouts  1.31 us (2%)
    pallas_call x1, Pallas kernels, per_device(): pl.pallas_call(own_kernel, out_shape=[pltpu.VMEM((BLOCKS, *plain), F32),...  59.2 us
    pallas_call x1, Pallas kernels, per_device(): pl.pallas_call(layout_kernel, out_shape=jax.ShapeDtypeStruct((BLOCKS, SLA...  8.73 us

profile of v1, /device:TPU:65, one launch (start us, length us, event | category | flops | bytes accessed | tf_op | source)
XLA Modules:
  0.0 69.3 jit_solution(15737347872640020101)
XLA Ops:
  0.0 0.0 copy-start.1
  0.0 0.0 copy-start
  0.0 1.3 %reshape.10.links = s32[48]{0:T(128)} reshape(s32[8,6]{1,0:T(8,128)} %param.5) | data formatting | bytes 384 | tf_op jit(solution)/shard_map/reshape | solution.py:526
  1.3 59.2 %shard_map.46 = (f32[8,32,64,128]{3,2,1,0:T(8,128)S(1)}, f32[2,32,80,128]{3,2,1,0:T(8,128)S(1)}, f32[2,2,6,32,128]{4,3,2,1,0:T(8,128)S(1)}, f32[2,8,128]{2,1,0:T(8,128)S(1)}) custom-call(f32[8,8,32,8,128]{4,3,2,1,0:T(8,128)} %bitcast.6, s32[48]{0:T(128)} %reshape.10.links, s32[8]{0:T(128)} %owner.3, s32[8]{0:T(128)} %slot.3), custom_call_target="tpu_custom_call" | custom-call | tf_op jit(solution)/shard_map/pallas_call | solution.py:535
  60.6 0.0 copy-done.1
  60.6 0.0 copy-done
  60.6 8.7 %shard_map.47 = f32[8,8,32,8,128]{4,3,2,1,0:T(8,128)} custom-call(f32[8,32,64,128]{3,2,1,0:T(8,128)S(1)} %get-tuple-element.9.stage, f32[2,32,80,128]{3,2,1,0:T(8,128)S(1)} %get-tuple-element.10.got, f32[2,2,6,32,128]{4,3,2,1,0:T(8,128)S(1)} %get-tuple-element.11.got_layers, f32[2,8,128]{2,1,0:T(8,128)S(1)} %get-tuple-element.12.got_marks, s32[8]{0:T(128)S(1)} %copy-done, ...), custom_call_target="tpu_custom_call" | custom-call | tf_op jit(solution)/shard_map/pallas_call | solution.py:566
Async XLA Ops:
  0.0 60.6 %copy-start.1 = (s32[8]{0:T(128)S(1)}, s32[8]{0:T(128)}, u32[]{:S(2)}) copy-start(s32[8]{0:T(128)} %slot.3) | copy-start | bytes 100
  0.0 60.6 %copy-start = (s32[8]{0:T(128)S(1)}, s32[8]{0:T(128)}, u32[]{:S(2)}) copy-start(s32[8]{0:T(128)} %owner.3) | copy-start | bytes 100

commit v2 on v1

--- a/solution.py
+++ b/solution.py
@@ -15,6 +15,9 @@
 PITCH = 80
 F32 = jnp.float32
 FACE = (32, LANES)
+HALF = 4
+FIRST, SECOND = 2, 5
+STEP = 2
 
 
 def masks_of():
@@ -99,7 +102,7 @@
     )
 
 
-def chemical_slab(masks, field, chem, side_mobility, z, halo, keep):
+def chemical_slab(masks, field, chem, side_mobility, z, halo):
     sides = shifted_sides(masks, field, z, halo)
     for k, values in enumerate(sides):
         side_mobility[k, eight(z), :] = mobility(values)
@@ -111,8 +114,6 @@
             total = ((a + b) + (c + d)) + (e + f)
             value = tile * (14.0 + tile * (4.0 * tile - 6.0)) - (total + total)
             chem[8 * xf + yf, rows, :] = value
-            if keep is not None and yf in (0, 7):
-                keep(xf, yf, value)
 
 
 def advance_slab(masks, field, chem, scaled, side_mobility, out, z, halo):
@@ -130,9 +131,33 @@
             out[tile, rows, :] = field[tile, rows, :] + flux
 
 
-def y_part(masks, tile, yf, z, held):
-    shift = lax.rem((z - (7 if yf else 0)) * 16 + LANES, LANES)
-    return jnp.where(masks["yc"] == z, turned(tile, shift), held)
+def y_faces(masks, block):
+    faces = []
+    for yf in (0, 7):
+        parts = []
+        for xf in range(4):
+            held = jnp.zeros((8, LANES), F32)
+            for z in range(SLABS):
+                tile = block[8 * xf + yf, slab(z), :]
+                held = jnp.where(masks["yc"] == z, turned(tile, (z - yf) * 16), held)
+            parts.append(held)
+        faces.append(jnp.concatenate(parts, 0))
+    return faces
+
+
+def add_y(masks, block, d, change):
+    yf = 7 if d == 2 else 0
+    where = masks["y_last" if d == 2 else "y_first"]
+    for xf in range(4):
+        for z in range(SLABS):
+            spread = turned(change[8 * xf : 8 * xf + 8], (yf - z) * 16)
+            tile = 8 * xf + yf
+            block[tile, slab(z), :] = block[tile, slab(z), :] + jnp.where(where, spread, 0.0)
+
+
+def add_z(block, d, change):
+    row = TOP + 63 if d == 4 else TOP
+    set_z_rows(block, row, z_rows(block, row) + change)
 
 
 def y_halo(face, side, xf, z):
@@ -178,7 +203,7 @@
 
 def own_kernel(
     c_hbm, links, owner, slot, stage, got, got_layers, got_marks,
-    field, chem, scaled, side_mobility, pay, y_c, z_c, y_u, z_u, sent_c, sent_u, came_c, came_u, packed, marks, table,
+    field, chem, scaled, side_mobility, pay, y_c, z_c, y_u, z_u, sent_c, sent_u, came_c, came_u, packed, marks, table, local, remote_face,
     load_sem, face_send, face_recv, block_send, block_recv, pack_send, pack_recv,
 ):
     me, upper, lower = place()
@@ -196,7 +221,7 @@
         pl.semaphore_signal(barrier, inc=1, device_id=device, device_id_type=MESH)
 
     def link(b, d):
-        return links[b * 6 + d]
+        return links[b, d]
 
     near_base = {2: 0, 3: 8, 4: 0, 5: 8}
     far_base = {2: 18, 3: 16, 4: 16, 5: 18}
@@ -214,8 +239,11 @@
         for b in range(BLOCKS):
             p = link(b, d)
             far = far_base[d] + ((p & 7) > least).astype(jnp.int32)
-            index = jnp.where((p >> 3) == me, near_base[d] + (p & 7), far)
-            table[b * 6 + d] = jnp.where(p < 0, own_base[d] + b, index)
+            own, near = own_base[d] + b, near_base[d] + (p & 7)
+            here = (p >> 3) == me
+            table[b * 6 + d] = jnp.where(p < 0, own, jnp.where(here, near, far))
+            local[b * 6 + d] = jnp.where((p >= 0) & here, near, own)
+            remote_face[b * 6 + d] = jnp.where((p >= 0) & ~here, far, own)
     moving, mark_right, mark_left = jnp.int32(0), jnp.int32(0), jnp.int32(0)
     for b in range(BLOCKS):
         goes_right, goes_left = owner[b] == me + 1, owner[b] == me - 1
@@ -235,67 +263,30 @@
             else:
                 pay[extra, tile] = values
 
-    @pl.loop(0, BLOCKS)
-    def _(b):
-        for xo in range(SLABS):
-            load(b, xo).wait()
-
-        @pl.loop(0, 8)
-        def _(k):
-            for q in range(2):
-                take_in(b, k // 2, (k % 2) * 2 + q)
+    def take_blocks(start, end):
+        @pl.loop(start, end)
+        def _(b):
+            @pl.loop(0, 8)
+            def _(k):
+                for q in range(2):
+                    take_in(b, k // 2, (k % 2) * 2 + q)
+
+    @pl.loop(0, BLOCKS * SLABS)
+    def _(i):
+        load(i // SLABS, i % SLABS).wait()
 
     @pl.loop(0, 8)
     def _(k):
         for q in range(2):
             take_in(moving, k // 2, (k % 2) * 2 + q, 0)
 
+    take_blocks(0, HALF)
+
     @pl.loop(0, TILES)
     def _(t):
         pay[1, t] = field[0, t, TOP : TOP + 64, :]
 
-    def z_faces(values, z_table):
-        @pl.loop(0, BLOCKS)
-        def _(b):
-            z_table[b] = z_rows(values.at[b], TOP)
-            z_table[BLOCKS + b] = z_rows(values.at[b], TOP + 63)
-
-    z_faces(field, z_c)
-
-    def keep_y(y_table, b, z):
-        def keep(xf, yf, value):
-            entry = BLOCKS + b if yf else b
-            y_table[entry, part(xf), :] = y_part(masks, value, yf, z, y_table[entry, part(xf), :])
-
-        return keep
-
-    @pl.loop(0, BLOCKS * SLABS)
-    def _(i):
-        b, z = i // SLABS, i % SLABS
-        keep = keep_y(y_c, b, z)
-        for xf in range(4):
-            for yf in (0, 7):
-                keep(xf, yf, field[b, 8 * xf + yf, slab(z), :])
-
     pl.semaphore_wait(barrier, 2)
-
-    def fill(message, y_table, z_table):
-        for side, (y_dir, z_dir) in enumerate(((2, 5), (3, 4))):
-            for k in range(2):
-                message[side, k] = y_table[picks[y_dir][k]]
-                message[side, 2 + k] = z_table[picks[z_dir][k]]
-
-    def face_copies(k, message, came):
-        return [
-            remote(message.at[side], came.at[side], face_send.at[k, side], face_recv.at[k, side], device)
-            for side, device in enumerate((upper, lower))
-        ]
-
-    def take(came, y_table, z_table):
-        for side in range(2):
-            for k in range(2):
-                y_table[16 + 2 * side + k] = came[side, k]
-                z_table[16 + 2 * side + k] = came[side, 2 + k]
 
     def block_copies(z):
         return [
@@ -306,6 +297,41 @@
             for side, device in enumerate((upper, lower))
         ]
 
+    def hand_on(start, end):
+        for z in range(start, end):
+            for copy in block_copies(z):
+                copy.start()
+
+    hand_on(0, FIRST)
+    take_blocks(HALF, BLOCKS)
+
+    def faces_of(values, y_table, z_table):
+        @pl.loop(0, BLOCKS)
+        def _(b):
+            z_table[b] = z_rows(values.at[b], TOP)
+            z_table[BLOCKS + b] = z_rows(values.at[b], TOP + 63)
+            y_table[b], y_table[BLOCKS + b] = y_faces(masks, values.at[b])
+
+    faces_of(field, y_c, z_c)
+
+    def fill(message, y_table, z_table):
+        for side, (y_dir, z_dir) in enumerate(((2, 5), (3, 4))):
+            for k in range(2):
+                message[side, k] = y_table[picks[y_dir][k]]
+                message[side, 2 + k] = z_table[picks[z_dir][k]]
+
+    def face_copies(k, message, came):
+        return [
+            remote(message.at[side], came.at[side], face_send.at[k, side], face_recv.at[k, side], device)
+            for side, device in enumerate((upper, lower))
+        ]
+
+    def take(came, y_table, z_table):
+        for side in range(2):
+            for k in range(2):
+                y_table[16 + 2 * side + k] = came[side, k]
+                z_table[16 + 2 * side + k] = came[side, 2 + k]
+
     def halo_of(values, y_table, b, z):
         rows = slab(z)
         open_high, open_low = link(b, 0) < 0, link(b, 1) < 0
@@ -317,13 +343,13 @@
                 return jnp.where(open_high, values[b, 24 + k, rows, :], turned(values[high, k, rows, :], 15))
             if side == 1:
                 return jnp.where(open_low, values[b, k, rows, :], turned(values[low, 24 + k, rows, :], -15))
-            return y_halo(y_table.at[table[b * 6 + side]], side, k, z)
+            return y_halo(y_table.at[local[b * 6 + side]], side, k, z)
 
         return halo
 
     def set_z(values, z_table, b, scale=None):
         for row, d in ((TOP + 64, 4), (TOP - 1, 5)):
-            layer = z_table[table[b * 6 + d]]
+            layer = z_table[local[b * 6 + d]]
             set_z_rows(values.at[b], row, layer)
             if scale is not None:
                 set_z_rows(scale.at[b], row, mobility(layer))
@@ -332,33 +358,38 @@
     first_faces = face_copies(0, sent_c, came_c)
     for copy in first_faces:
         copy.start()
-    early = 3
-    for z in range(early):
-        for copy in block_copies(z):
-            copy.start()
+    hand_on(FIRST, SECOND)
+
+    @pl.loop(0, BLOCKS)
+    def _(b):
+        set_z(field, z_c, b, scaled)
+
+    @pl.loop(0, BLOCKS * SLABS // STEP)
+    def _(i):
+        b = i // (SLABS // STEP)
+        for q in range(STEP):
+            z = i % (SLABS // STEP) * STEP + q
+            chemical_slab(masks, field.at[b], chem.at[b], side_mobility.at[b], z, halo_of(field, y_c, b, z))
+
     for copy in first_faces:
         copy.wait_recv()
     take(came_c, y_c, z_c)
 
     @pl.loop(0, BLOCKS)
     def _(b):
-        set_z(field, z_c, b, scaled)
-
-    @pl.loop(0, BLOCKS * SLABS)
-    def _(i):
-        b, z = i // SLABS, i % SLABS
-        chemical_slab(
-            masks, field.at[b], chem.at[b], side_mobility.at[b], z, halo_of(field, y_c, b, z), keep_y(y_u, b, z)
-        )
-
-    z_faces(chem, z_u)
+        for d in (2, 3):
+            own = y_c[own_base[d] + b]
+            add_y(masks, chem.at[b], d, -2.0 * (y_c[remote_face[b * 6 + d]] - own))
+        for d in (4, 5):
+            own = z_c[own_base[d] + b]
+            add_z(chem.at[b], d, -2.0 * (z_c[remote_face[b * 6 + d]] - own))
+
+    faces_of(chem, y_u, z_u)
     fill(sent_u, y_u, z_u)
     second_faces = face_copies(1, sent_u, came_u)
     for copy in second_faces:
         copy.start()
-    for z in range(early, SLABS):
-        for copy in block_copies(z):
-            copy.start()
+    hand_on(SECOND, SLABS)
 
     def pack(k, values, y_table, z_table):
         for side, b in ((0, moving), (1, 0)):
@@ -380,14 +411,24 @@
                         )
 
     pack(0, field, y_c, z_c)
+
+    @pl.loop(0, BLOCKS)
+    def _(b):
+        set_z(chem, z_u, b)
+
+    @pl.loop(0, BLOCKS * SLABS // STEP)
+    def _(i):
+        b = i // (SLABS // STEP)
+        for q in range(STEP):
+            z = i % (SLABS // STEP) * STEP + q
+            advance_slab(
+                masks, field.at[b], chem.at[b], scaled.at[b], side_mobility.at[b], field.at[b], z,
+                halo_of(chem, y_u, b, z),
+            )
+
     for copy in second_faces:
         copy.wait_recv()
     take(came_u, y_u, z_u)
-
-    @pl.loop(0, BLOCKS)
-    def _(b):
-        set_z(chem, z_u, b)
-
     pack(1, chem, y_u, z_u)
     pack_copies = []
     for side, device in enumerate((upper, lower)):
@@ -400,13 +441,17 @@
     for copy in pack_copies:
         copy.start()
 
-    @pl.loop(0, BLOCKS * SLABS)
-    def _(i):
-        b, z = i // SLABS, i % SLABS
-        advance_slab(
-            masks, field.at[b], chem.at[b], scaled.at[b], side_mobility.at[b], field.at[b], z,
-            halo_of(chem, y_u, b, z),
-        )
+    def far_flux(field_table, chem_table, b, d):
+        own, far = own_base[d] + b, remote_face[b * 6 + d]
+        passing = mobility(field_table[own]) + mobility(field_table[far])
+        return passing * (chem_table[far] - chem_table[own])
+
+    @pl.loop(0, BLOCKS)
+    def _(b):
+        for d in (2, 3):
+            add_y(masks, field.at[b], d, far_flux(y_c, y_u, b, d))
+        for d in (4, 5):
+            add_z(field.at[b], d, far_flux(z_c, z_u, b, d))
 
     @pl.loop(0, BLOCKS * 8)
     def _(i):
@@ -486,7 +531,7 @@
 
             @pl.loop(0, SLABS)
             def _(z):
-                chemical_slab(masks, arrived, chem, side_mobility, z, halo_of(0, z), None)
+                chemical_slab(masks, arrived, chem, side_mobility, z, halo_of(0, z))
 
             @pl.loop(0, SLABS)
             def _(z):
@@ -523,7 +568,6 @@
 
 def per_device(concentration, neighbour, new_owner, new_slot):
     tiles = concentration.reshape(BLOCKS, SLABS, 8, 32, LANES).transpose(0, 1, 3, 2, 4)
-    links = neighbour.reshape(BLOCKS * 6)
     anywhere = pl.BlockSpec(memory_space=pl.ANY)
     scalars = pl.BlockSpec(memory_space=pltpu.SMEM)
     vector = pl.BlockSpec(memory_space=pltpu.VMEM)
@@ -550,7 +594,7 @@
             *[pltpu.VMEM((2, 4, *FACE), F32)] * 4,
             pltpu.VMEM((2, 2, 6, *FACE), F32),
             pltpu.VMEM((2, 8, LANES), F32),
-            pltpu.SMEM((BLOCKS * 6,), jnp.int32),
+            *[pltpu.SMEM((BLOCKS * 6,), jnp.int32)] * 3,
             dma((BLOCKS, SLABS)),
             dma((2, 2)),
             dma((2, 2)),
@@ -562,7 +606,7 @@
         compiler_params=pltpu.CompilerParams(
             collective_id=0, has_side_effects=True, vmem_limit_bytes=48 << 20
         ),
-    )(tiles, links, new_owner, new_slot)
+    )(tiles, neighbour, new_owner, new_slot)
     out = pl.pallas_call(
         layout_kernel,
         out_shape=jax.ShapeDtypeStruct((BLOCKS, SLABS, 32, 8, LANES), F32),

time: 70.4 us -> 56.1 us (0.80)
  the two profiles are of different devices: /device:TPU:65 before, /device:TPU:0 now
where the time goes in v2:
time: 56.1 us; the launch traced here: 55.9 us
  Pallas kernels  55.9 us (100%)
    pallas_call x1, Pallas kernels, per_device(): pl.pallas_call(own_kernel, out_shape=[pltpu.VMEM((BLOCKS, *plain), F32),...  51.3 us
    pallas_call x1, Pallas kernels, per_device(): pl.pallas_call(layout_kernel, out_shape=jax.ShapeDtypeStruct((BLOCKS, SLA...  4.63 us

profile of v2, /device:TPU:0, one launch (start us, length us, event | category | flops | bytes accessed | tf_op | source)
XLA Modules:
  0.0 55.9 jit_solution(3913720276749668348)
XLA Ops:
  0.0 0.0 copy-start.1
  0.0 0.0 copy-start
  0.0 51.3 %shard_map.46 = (f32[8,32,64,128]{3,2,1,0:T(8,128)S(1)}, f32[2,32,80,128]{3,2,1,0:T(8,128)S(1)}, f32[2,2,6,32,128]{4,3,2,1,0:T(8,128)S(1)}, f32[2,8,128]{2,1,0:T(8,128)S(1)}) custom-call(f32[8,8,32,8,128]{4,3,2,1,0:T(8,128)} %bitcast.6, s32[8,6]{1,0:T(8,128)} %links.1, s32[8]{0:T(128)} %owner.3, s32[8]{0:T(128)} %slot.3), custom_call_target="tpu_custom_call" | custom-call | tf_op jit(solution)/shard_map/pallas_call | solution.py:579
  51.3 0.0 copy-done.1
  51.3 0.0 copy-done
  51.3 4.6 %shard_map.47 = f32[8,8,32,8,128]{4,3,2,1,0:T(8,128)} custom-call(f32[8,32,64,128]{3,2,1,0:T(8,128)S(1)} %get-tuple-element.9.stage, f32[2,32,80,128]{3,2,1,0:T(8,128)S(1)} %get-tuple-element.10.got, f32[2,2,6,32,128]{4,3,2,1,0:T(8,128)S(1)} %get-tuple-element.11.got_layers, f32[2,8,128]{2,1,0:T(8,128)S(1)} %get-tuple-element.12.got_marks, s32[8]{0:T(128)S(1)} %copy-done, ...), custom_call_target="tpu_custom_call" | custom-call | tf_op jit(solution)/shard_map/pallas_call | solution.py:610
Async XLA Ops:
  0.0 51.3 %copy-start.1 = (s32[8]{0:T(128)S(1)}, s32[8]{0:T(128)}, u32[]{:S(2)}) copy-start(s32[8]{0:T(128)} %slot.3) | copy-start | bytes 100
  0.0 51.3 %copy-start = (s32[8]{0:T(128)S(1)}, s32[8]{0:T(128)}, u32[]{:S(2)}) copy-start(s32[8]{0:T(128)} %owner.3) | copy-start | bytes 100

commit v3 on v2

--- a/solution.py
+++ b/solution.py
@@ -15,9 +15,8 @@
 PITCH = 80
 F32 = jnp.float32
 FACE = (32, LANES)
-HALF = 4
-FIRST, SECOND = 2, 5
-STEP = 2
+FIRST, SECOND = 3, 6
+STEP = 4
 
 
 def masks_of():
@@ -49,7 +48,7 @@
 def slab(z, offset=0):
     if offset:
         return pl.ds(TOP + 8 * z + offset, 8)
-    return pl.ds(pl.multiple_of(TOP + 8 * z, 8), 8)
+    return pl.ds(TOP + 8 * z if isinstance(z, int) else pl.multiple_of(TOP + 8 * z, 8), 8)
 
 
 def eight(z):
@@ -192,7 +191,7 @@
     def coordinates(device):
         return (device // minor, lax.rem(device, minor))
 
-    return me, coordinates(upper), coordinates(lower)
+    return size, me, coordinates(upper), coordinates(lower)
 
 
 def remote(source, target, send, receive, device):
@@ -204,9 +203,9 @@
 def own_kernel(
     c_hbm, links, owner, slot, stage, got, got_layers, got_marks,
     field, chem, scaled, side_mobility, pay, y_c, z_c, y_u, z_u, sent_c, sent_u, came_c, came_u, packed, marks, table, local, remote_face,
-    load_sem, face_send, face_recv, block_send, block_recv, pack_send, pack_recv,
+    load_sem, face_send, face_recv, block_send, block_recv, pack_send, pack_recv, lower_here,
 ):
-    me, upper, lower = place()
+    size, me, upper, lower = place()
     masks = masks_of()
 
     def load(b, xo):
@@ -217,8 +216,7 @@
         load(i // SLABS, i % SLABS).start()
 
     barrier = pltpu.get_barrier_semaphore()
-    for device in (upper, lower):
-        pl.semaphore_signal(barrier, inc=1, device_id=device, device_id_type=MESH)
+    pl.semaphore_signal(barrier, inc=1, device_id=lower, device_id_type=MESH)
 
     def link(b, d):
         return links[b, d]
@@ -266,44 +264,49 @@
     def take_blocks(start, end):
         @pl.loop(start, end)
         def _(b):
-            @pl.loop(0, 8)
+            @pl.loop(0, 4)
             def _(k):
-                for q in range(2):
-                    take_in(b, k // 2, (k % 2) * 2 + q)
+                for q in range(4):
+                    take_in(b, k, q)
+
+    def block_copy(side, z):
+        return remote(
+            pay.at[side, :, eight(z), :], got.at[side, :, slab(z), :],
+            block_send.at[side, z], block_recv.at[side, z], (upper, lower)[side],
+        )
+
+    has_upper, has_lower = me < size - 1, me > 0
+
+    def hand_on(side, start, end):
+        @pl.when((has_upper, has_lower)[side])
+        def _():
+            for z in range(start, end):
+                block_copy(side, z).start()
 
     @pl.loop(0, BLOCKS * SLABS)
     def _(i):
         load(i // SLABS, i % SLABS).wait()
 
-    @pl.loop(0, 8)
+    @pl.loop(0, 4)
     def _(k):
-        for q in range(2):
-            take_in(moving, k // 2, (k % 2) * 2 + q, 0)
-
-    take_blocks(0, HALF)
+        for q in range(4):
+            take_in(moving, k, q, 0)
+
+    pl.semaphore_wait(barrier, 1)
+    pl.semaphore_signal(lower_here, inc=1, device_id=upper, device_id_type=MESH)
+    hand_on(0, 0, FIRST)
+    take_blocks(0, 1)
 
     @pl.loop(0, TILES)
     def _(t):
         pay[1, t] = field[0, t, TOP : TOP + 64, :]
 
-    pl.semaphore_wait(barrier, 2)
-
-    def block_copies(z):
-        return [
-            remote(
-                pay.at[side, :, eight(z), :], got.at[side, :, slab(z), :],
-                block_send.at[side, z], block_recv.at[side, z], device,
-            )
-            for side, device in enumerate((upper, lower))
-        ]
-
-    def hand_on(start, end):
-        for z in range(start, end):
-            for copy in block_copies(z):
-                copy.start()
-
-    hand_on(0, FIRST)
-    take_blocks(HALF, BLOCKS)
+    @pl.when(has_lower)
+    def _():
+        pl.semaphore_wait(lower_here, 1)
+
+    hand_on(1, 0, FIRST)
+    take_blocks(1, BLOCKS)
 
     def faces_of(values, y_table, z_table):
         @pl.loop(0, BLOCKS)
@@ -355,10 +358,16 @@
                 set_z_rows(scale.at[b], row, mobility(layer))
 
     fill(sent_c, y_c, z_c)
+
+    @pl.when(me == 0)
+    def _():
+        pl.semaphore_wait(lower_here, 1)
+
     first_faces = face_copies(0, sent_c, came_c)
     for copy in first_faces:
         copy.start()
-    hand_on(FIRST, SECOND)
+    for side in range(2):
+        hand_on(side, FIRST, SECOND)
 
     @pl.loop(0, BLOCKS)
     def _(b):
@@ -389,7 +398,8 @@
     second_faces = face_copies(1, sent_u, came_u)
     for copy in second_faces:
         copy.start()
-    hand_on(SECOND, SLABS)
+    for side in range(2):
+        hand_on(side, SECOND, SLABS)
 
     def pack(k, values, y_table, z_table):
         for side, b in ((0, moving), (1, 0)):
@@ -398,17 +408,18 @@
             for d in (4, 5):
                 packed[side, k, d] = z_table[table[b * 6 + d]]
 
-            @pl.loop(0, SLABS)
-            def _(z, side=side, b=b):
-                halo = halo_of(values, y_table, b, z)
-                for d in range(2):
-                    for yf in range(8):
-                        spot = (yf & 1) * 8 + z
-                        shift = lax.rem(spot - (0 if d else 15) + LANES, LANES)
-                        held = packed[side, k, d, part(yf >> 1), :]
-                        packed[side, k, d, part(yf >> 1), :] = jnp.where(
-                            masks["xc"] == spot, turned(halo(d, yf), shift), held
-                        )
+            for d in range(2):
+
+                @pl.loop(0, 4)
+                def _(v, side=side, b=b, d=d):
+                    held = jnp.zeros((8, LANES), F32)
+                    for z in range(SLABS):
+                        halo = halo_of(values, y_table, b, z)
+                        for e in range(2):
+                            spot = 8 * e + z
+                            moved = turned(halo(d, 2 * v + e), spot - (0 if d else 15))
+                            held = jnp.where(masks["xc"] == spot, moved, held)
+                    packed[side, k, d, eight(v), :] = held
 
     pack(0, field, y_c, z_c)
 
@@ -430,16 +441,20 @@
         copy.wait_recv()
     take(came_u, y_u, z_u)
     pack(1, chem, y_u, z_u)
-    pack_copies = []
-    for side, device in enumerate((upper, lower)):
-        pack_copies.append(
-            remote(packed.at[side], got_layers.at[side], pack_send.at[0, side], pack_recv.at[0, side], device)
-        )
-        pack_copies.append(
-            remote(marks.at[side], got_marks.at[side], pack_send.at[1, side], pack_recv.at[1, side], device)
-        )
-    for copy in pack_copies:
-        copy.start()
+
+    def pack_copies(side):
+        device = (upper, lower)[side]
+        return [
+            remote(packed.at[side], got_layers.at[side], pack_send.at[0, side], pack_recv.at[0, side], device),
+            remote(marks.at[side], got_marks.at[side], pack_send.at[1, side], pack_recv.at[1, side], device),
+        ]
+
+    for side in range(2):
+
+        @pl.when((has_upper, has_lower)[side])
+        def _(side=side):
+            for copy in pack_copies(side):
+                copy.start()
 
     def far_flux(field_table, chem_table, b, d):
         own, far = own_base[d] + b, remote_face[b * 6 + d]
@@ -453,17 +468,24 @@
         for d in (4, 5):
             add_z(field.at[b], d, far_flux(z_c, z_u, b, d))
 
-    @pl.loop(0, BLOCKS * 8)
+    @pl.loop(0, BLOCKS * 4)
     def _(i):
-        b, k = i // 8, i % 8
-        for q in range(2):
-            group_out(stage.at[b], k // 2, (k % 2) * 2 + q, field.at[b])
-
-    for copy in pack_copies:
-        copy.wait()
-    for z in range(SLABS):
-        for copy in block_copies(z):
-            copy.wait()
+        b, k = i // 4, i % 4
+        for q in range(4):
+            group_out(stage.at[b], k, q, field.at[b])
+
+    for side in range(2):
+
+        @pl.when((has_upper, has_lower)[side])
+        def _(side=side):
+            for copy in pack_copies(side) + [block_copy(side, z) for z in range(SLABS)]:
+                copy.wait_send()
+
+        @pl.when((has_lower, has_upper)[side])
+        def _(side=side):
+            for copy in pack_copies(side) + [block_copy(side, z) for z in range(SLABS)]:
+                copy.wait_recv()
+
     for copy in first_faces + second_faces:
         copy.wait_send()
 
@@ -472,7 +494,7 @@
     stage, got, got_layers, got_marks, owner, slot, out,
     arrived, scaled, chem, stepped, side_mobility, final, zeros, keep_sem, zero_sem, new_sem,
 ):
-    me, _, _ = place()
+    size, me, _, _ = place()
     masks = masks_of()
 
     def keep_copy(b, xo):
@@ -493,7 +515,10 @@
             for xo in range(SLABS):
                 keep_copy(b, xo).start()
 
-    places = [jnp.max(got_marks[side]).astype(jnp.int32) for side in range(2)]
+    places = [
+        jnp.where(there, jnp.max(got_marks[side]).astype(jnp.int32), 0)
+        for side, there in enumerate((me > 0, me < size - 1))
+    ]
     count = kept
     for target in places:
         count = count + (target > 0).astype(jnp.int32)
@@ -602,6 +627,7 @@
             dma((2, SLABS)),
             dma((2, 2)),
             dma((2, 2)),
+            pltpu.SemaphoreType.REGULAR,
         ],
         compiler_params=pltpu.CompilerParams(
             collective_id=0, has_side_effects=True, vmem_limit_bytes=48 << 20

time: 56.1 us -> 57.2 us (1.020)
  the two profiles are of different devices: /device:TPU:0 before, /device:TPU:65 now
where the time goes in v3:
time: 57.2 us; the launch traced here: 57.1 us
  Pallas kernels  57 us (100%)
    pallas_call x1, Pallas kernels, per_device(): pl.pallas_call(own_kernel, out_shape=[pltpu.VMEM((BLOCKS, *plain), F32),...  48.3 us
    pallas_call x1, Pallas kernels, per_device(): pl.pallas_call(layout_kernel, out_shape=jax.ShapeDtypeStruct((BLOCKS, SLA...  8.73 us

profile of v3, /device:TPU:65, one launch (start us, length us, event | category | flops | bytes accessed | tf_op | source)
XLA Modules:
  0.0 57.1 jit_solution(9884586112529303363)
XLA Ops:
  0.0 0.0 copy-start.1
  0.0 0.0 copy-start
  0.0 48.3 %shard_map.46 = (f32[8,32,64,128]{3,2,1,0:T(8,128)S(1)}, f32[2,32,80,128]{3,2,1,0:T(8,128)S(1)}, f32[2,2,6,32,128]{4,3,2,1,0:T(8,128)S(1)}, f32[2,8,128]{2,1,0:T(8,128)S(1)}) custom-call(f32[8,8,32,8,128]{4,3,2,1,0:T(8,128)} %bitcast.6, s32[8,6]{1,0:T(8,128)} %links.1, s32[8]{0:T(128)} %owner.3, s32[8]{0:T(128)} %slot.3), custom_call_target="tpu_custom_call" | custom-call | tf_op jit(solution)/shard_map/pallas_call | solution.py:604
  48.3 0.0 copy-done.1
  48.3 0.0 copy-done
  48.3 8.7 %shard_map.47 = f32[8,8,32,8,128]{4,3,2,1,0:T(8,128)} custom-call(f32[8,32,64,128]{3,2,1,0:T(8,128)S(1)} %get-tuple-element.9.stage, f32[2,32,80,128]{3,2,1,0:T(8,128)S(1)} %get-tuple-element.10.got, f32[2,2,6,32,128]{4,3,2,1,0:T(8,128)S(1)} %get-tuple-element.11.got_layers, f32[2,8,128]{2,1,0:T(8,128)S(1)} %get-tuple-element.12.got_marks, s32[8]{0:T(128)S(1)} %copy-done, ...), custom_call_target="tpu_custom_call" | custom-call | tf_op jit(solution)/shard_map/pallas_call | solution.py:636
Async XLA Ops:
  0.0 48.3 %copy-start.1 = (s32[8]{0:T(128)S(1)}, s32[8]{0:T(128)}, u32[]{:S(2)}) copy-start(s32[8]{0:T(128)} %slot.3) | copy-start | bytes 100
  0.0 48.3 %copy-start = (s32[8]{0:T(128)S(1)}, s32[8]{0:T(128)}, u32[]{:S(2)}) copy-start(s32[8]{0:T(128)} %owner.3) | copy-start | bytes 100

commit v4 on v3

--- a/solution.py
+++ b/solution.py
@@ -15,8 +15,9 @@
 PITCH = 80
 F32 = jnp.float32
 FACE = (32, LANES)
-FIRST, SECOND = 3, 6
+AFTER = (2, 3, 4, 5, 7, 8)
 STEP = 4
+SPLIT = 4
 
 
 def masks_of():
@@ -294,7 +295,7 @@
 
     pl.semaphore_wait(barrier, 1)
     pl.semaphore_signal(lower_here, inc=1, device_id=upper, device_id_type=MESH)
-    hand_on(0, 0, FIRST)
+    hand_on(0, 0, AFTER[0])
     take_blocks(0, 1)
 
     @pl.loop(0, TILES)
@@ -305,8 +306,15 @@
     def _():
         pl.semaphore_wait(lower_here, 1)
 
-    hand_on(1, 0, FIRST)
-    take_blocks(1, BLOCKS)
+    hand_on(1, 0, AFTER[0])
+
+    def hand_more(k):
+        for side in range(2):
+            hand_on(side, AFTER[k - 1], AFTER[k])
+
+    take_blocks(1, 5)
+    hand_more(1)
+    take_blocks(5, BLOCKS)
 
     def faces_of(values, y_table, z_table):
         @pl.loop(0, BLOCKS)
@@ -366,19 +374,23 @@
     first_faces = face_copies(0, sent_c, came_c)
     for copy in first_faces:
         copy.start()
-    for side in range(2):
-        hand_on(side, FIRST, SECOND)
+    hand_more(2)
 
     @pl.loop(0, BLOCKS)
     def _(b):
         set_z(field, z_c, b, scaled)
 
-    @pl.loop(0, BLOCKS * SLABS // STEP)
-    def _(i):
-        b = i // (SLABS // STEP)
-        for q in range(STEP):
-            z = i % (SLABS // STEP) * STEP + q
-            chemical_slab(masks, field.at[b], chem.at[b], side_mobility.at[b], z, halo_of(field, y_c, b, z))
+    def chemical_blocks(start, end):
+        @pl.loop(start * (SLABS // STEP), end * (SLABS // STEP))
+        def _(i):
+            b = i // (SLABS // STEP)
+            for q in range(STEP):
+                z = i % (SLABS // STEP) * STEP + q
+                chemical_slab(masks, field.at[b], chem.at[b], side_mobility.at[b], z, halo_of(field, y_c, b, z))
+
+    chemical_blocks(0, 4)
+    hand_more(3)
+    chemical_blocks(4, BLOCKS)
 
     for copy in first_faces:
         copy.wait_recv()
@@ -398,8 +410,7 @@
     second_faces = face_copies(1, sent_u, came_u)
     for copy in second_faces:
         copy.start()
-    for side in range(2):
-        hand_on(side, SECOND, SLABS)
+    hand_more(4)
 
     def pack(k, values, y_table, z_table):
         for side, b in ((0, moving), (1, 0)):
@@ -408,18 +419,24 @@
             for d in (4, 5):
                 packed[side, k, d] = z_table[table[b * 6 + d]]
 
-            for d in range(2):
-
-                @pl.loop(0, 4)
-                def _(v, side=side, b=b, d=d):
-                    held = jnp.zeros((8, LANES), F32)
-                    for z in range(SLABS):
-                        halo = halo_of(values, y_table, b, z)
-                        for e in range(2):
-                            spot = 8 * e + z
-                            moved = turned(halo(d, 2 * v + e), spot - (0 if d else 15))
-                            held = jnp.where(masks["xc"] == spot, moved, held)
-                    packed[side, k, d, eight(v), :] = held
+
+        @pl.loop(0, 4)
+        def _(v):
+            for side, b in ((0, moving), (1, 0)):
+                for d in range(2):
+                    closed = link(b, d) < 0
+                    beside = jnp.where(closed, b, link(b, d) & 7)
+                    inner, outer = (24, 0) if d == 0 else (0, 24)
+                    place_in, place_out = (15, 0) if d == 0 else (0, 15)
+                    mine, other = jnp.zeros((8, LANES), F32), jnp.zeros((8, LANES), F32)
+                    for e in range(2):
+                        for z in range(SLABS):
+                            spot, k8 = 8 * e + z, 2 * v + e
+                            there = masks["xc"] == spot
+                            own = turned(values[b, inner + k8, slab(z), :], spot - place_in)
+                            far = turned(values[beside, outer + k8, slab(z), :], spot - place_out)
+                            mine, other = jnp.where(there, own, mine), jnp.where(there, far, other)
+                    packed[side, k, d, eight(v), :] = jnp.where(closed, mine, other)
 
     pack(0, field, y_c, z_c)
 
@@ -427,15 +444,19 @@
     def _(b):
         set_z(chem, z_u, b)
 
-    @pl.loop(0, BLOCKS * SLABS // STEP)
-    def _(i):
-        b = i // (SLABS // STEP)
-        for q in range(STEP):
-            z = i % (SLABS // STEP) * STEP + q
-            advance_slab(
-                masks, field.at[b], chem.at[b], scaled.at[b], side_mobility.at[b], field.at[b], z,
-                halo_of(chem, y_u, b, z),
-            )
+    def advance_blocks(start, end):
+        @pl.loop(start * (SLABS // STEP), end * (SLABS // STEP))
+        def _(i):
+            b = i // (SLABS // STEP)
+            for q in range(STEP):
+                z = i % (SLABS // STEP) * STEP + q
+                advance_slab(
+                    masks, field.at[b], chem.at[b], scaled.at[b], side_mobility.at[b], field.at[b], z,
+                    halo_of(chem, y_u, b, z),
+                )
+
+    advance_blocks(0, SPLIT)
+    hand_more(5)
 
     for copy in second_faces:
         copy.wait_recv()
@@ -455,6 +476,8 @@
         def _(side=side):
             for copy in pack_copies(side):
                 copy.start()
+
+    advance_blocks(SPLIT, BLOCKS)
 
     def far_flux(field_table, chem_table, b, d):
         own, far = own_base[d] + b, remote_face[b * 6 + d]
@@ -554,18 +577,22 @@
                 set_z_rows(scaled, row, mobility(layers[0, d]))
                 set_z_rows(chem, row, layers[1, d])
 
-            @pl.loop(0, SLABS)
-            def _(z):
-                chemical_slab(masks, arrived, chem, side_mobility, z, halo_of(0, z))
-
-            @pl.loop(0, SLABS)
-            def _(z):
-                advance_slab(masks, arrived, chem, scaled, side_mobility, stepped, z, halo_of(1, z))
-
-            @pl.loop(0, 8)
+            @pl.loop(0, SLABS // STEP)
+            def _(i):
+                for q in range(STEP):
+                    z = i * STEP + q
+                    chemical_slab(masks, arrived, chem, side_mobility, z, halo_of(0, z))
+
+            @pl.loop(0, SLABS // STEP)
+            def _(i):
+                for q in range(STEP):
+                    z = i * STEP + q
+                    advance_slab(masks, arrived, chem, scaled, side_mobility, stepped, z, halo_of(1, z))
+
+            @pl.loop(0, 4)
             def _(k):
-                for q in range(2):
-                    group_out(final.at[side], k // 2, (k % 2) * 2 + q, stepped)
+                for q in range(4):
+                    group_out(final.at[side], k, q, stepped)
 
             for xo in range(SLABS):
                 new_copy(side, xo).start()

time: 57.2 us -> 52.6 us (0.920)
  Pallas kernels: 57 us -> 52.4 us
    pallas_call x1, Pallas kernels: 48.3 us -> 45.2 us  [per_device(): pl.pallas_call(own_kernel, out_shape=[pltpu.VMEM((BLOCKS, *plain), F32),...]
    pallas_call x1, Pallas kernels: 8.73 us -> 7.26 us  [per_device(): pl.pallas_call(layout_kernel, out_shape=jax.ShapeDtypeStruct((BLOCKS, SLA...]
where the time goes in v4:
time: 52.6 us; the launch traced here: 52.5 us
  Pallas kernels  52.4 us (100%)
    pallas_call x1, Pallas kernels, per_device(): pl.pallas_call(own_kernel, out_shape=[pltpu.VMEM((BLOCKS, *plain), F32),...  45.2 us
    pallas_call x1, Pallas kernels, per_device(): pl.pallas_call(layout_kernel, out_shape=jax.ShapeDtypeStruct((BLOCKS, SLA...  7.26 us

profile of v4, /device:TPU:65, one launch (start us, length us, event | category | flops | bytes accessed | tf_op | source)
XLA Modules:
  0.0 52.5 jit_solution(1819161887824550830)
XLA Ops:
  0.0 0.0 copy-start.1
  0.0 0.0 copy-start
  0.0 45.2 %shard_map.46 = (f32[8,32,64,128]{3,2,1,0:T(8,128)S(1)}, f32[2,32,80,128]{3,2,1,0:T(8,128)S(1)}, f32[2,2,6,32,128]{4,3,2,1,0:T(8,128)S(1)}, f32[2,8,128]{2,1,0:T(8,128)S(1)}) custom-call(f32[8,8,32,8,128]{4,3,2,1,0:T(8,128)} %bitcast.6, s32[8,6]{1,0:T(8,128)} %links.1, s32[8]{0:T(128)} %owner.3, s32[8]{0:T(128)} %slot.3), custom_call_target="tpu_custom_call" | custom-call | tf_op jit(solution)/shard_map/pallas_call | solution.py:631
  45.2 0.0 copy-done.1
  45.2 0.0 copy-done
  45.2 7.3 %shard_map.47 = f32[8,8,32,8,128]{4,3,2,1,0:T(8,128)} custom-call(f32[8,32,64,128]{3,2,1,0:T(8,128)S(1)} %get-tuple-element.9.stage, f32[2,32,80,128]{3,2,1,0:T(8,128)S(1)} %get-tuple-element.10.got, f32[2,2,6,32,128]{4,3,2,1,0:T(8,128)S(1)} %get-tuple-element.11.got_layers, f32[2,8,128]{2,1,0:T(8,128)S(1)} %get-tuple-element.12.got_marks, s32[8]{0:T(128)S(1)} %copy-done, ...), custom_call_target="tpu_custom_call" | custom-call | tf_op jit(solution)/shard_map/pallas_call | solution.py:663
Async XLA Ops:
  0.0 45.2 %copy-start.1 = (s32[8]{0:T(128)S(1)}, s32[8]{0:T(128)}, u32[]{:S(2)}) copy-start(s32[8]{0:T(128)} %slot.3) | copy-start | bytes 100
  0.0 45.2 %copy-start = (s32[8]{0:T(128)S(1)}, s32[8]{0:T(128)}, u32[]{:S(2)}) copy-start(s32[8]{0:T(128)} %owner.3) | copy-start | bytes 100

commit v5 on v4

--- a/solution.py
+++ b/solution.py
@@ -15,9 +15,9 @@
 PITCH = 80
 F32 = jnp.float32
 FACE = (32, LANES)
-AFTER = (2, 3, 4, 5, 7, 8)
+AFTER = (2, 3, 4, 6, 8, 8)
 STEP = 4
-SPLIT = 4
+SPLIT = 5
 
 
 def masks_of():

time: 52.6 us -> 50.2 us (0.954)
  the two profiles are of different devices: /device:TPU:65 before, /device:TPU:95 now
where the time goes in v5:
time: 50.2 us; the launch traced here: 50 us
  Pallas kernels  50 us (100%)
    pallas_call x1, Pallas kernels, per_device(): pl.pallas_call(own_kernel, out_shape=[pltpu.VMEM((BLOCKS, *plain), F32),...  42.7 us
    pallas_call x1, Pallas kernels, per_device(): pl.pallas_call(layout_kernel, out_shape=jax.ShapeDtypeStruct((BLOCKS, SLA...  7.26 us

profile of v5, /device:TPU:95, one launch (start us, length us, event | category | flops | bytes accessed | tf_op | source)
XLA Modules:
  0.0 50.0 jit_solution(8073329891635254943)
XLA Ops:
  0.0 0.0 copy-start.1
  0.0 0.0 copy-start
  0.0 42.7 %shard_map.46 = (f32[8,32,64,128]{3,2,1,0:T(8,128)S(1)}, f32[2,32,80,128]{3,2,1,0:T(8,128)S(1)}, f32[2,2,6,32,128]{4,3,2,1,0:T(8,128)S(1)}, f32[2,8,128]{2,1,0:T(8,128)S(1)}) custom-call(f32[8,8,32,8,128]{4,3,2,1,0:T(8,128)} %bitcast.6, s32[8,6]{1,0:T(8,128)} %links.1, s32[8]{0:T(128)} %owner.3, s32[8]{0:T(128)} %slot.3), custom_call_target="tpu_custom_call" | custom-call | tf_op jit(solution)/shard_map/pallas_call | solution.py:631
  42.7 0.0 copy-done.1
  42.7 0.0 copy-done
  42.8 7.3 %shard_map.47 = f32[8,8,32,8,128]{4,3,2,1,0:T(8,128)} custom-call(f32[8,32,64,128]{3,2,1,0:T(8,128)S(1)} %get-tuple-element.9.stage, f32[2,32,80,128]{3,2,1,0:T(8,128)S(1)} %get-tuple-element.10.got, f32[2,2,6,32,128]{4,3,2,1,0:T(8,128)S(1)} %get-tuple-element.11.got_layers, f32[2,8,128]{2,1,0:T(8,128)S(1)} %get-tuple-element.12.got_marks, s32[8]{0:T(128)S(1)} %copy-done, ...), custom_call_target="tpu_custom_call" | custom-call | tf_op jit(solution)/shard_map/pallas_call | solution.py:663
Async XLA Ops:
  0.0 42.7 %copy-start.1 = (s32[8]{0:T(128)S(1)}, s32[8]{0:T(128)}, u32[]{:S(2)}) copy-start(s32[8]{0:T(128)} %slot.3) | copy-start | bytes 100
  0.0 42.7 %copy-start = (s32[8]{0:T(128)S(1)}, s32[8]{0:T(128)}, u32[]{:S(2)}) copy-start(s32[8]{0:T(128)} %owner.3) | copy-start | bytes 100
